TPU v7x, 768 devices: a whole 4x8x12 slice. The times are simulated.
768 devices in a mesh: dp: 12 (over z), fold: 4 (over x), tensor: 16 (over y, core).
Axes of the slice: x: 4, y: 8, z: 12, core: 2. Of those that a mesh axis runs over, the one named last changes fastest.
Arguments:
- attn_heads: bfloat16 [24576, 4096], P(('dp', 'fold'), 'tensor'), may hold values from -6 to 6
- w_out: bfloat16 [4096, 2048], P('tensor'), may hold values from -0.09375 to 0.09375
- residual: bfloat16 [24576, 2048], P(('dp', 'fold', 'tensor')), may hold values from -6 to 6
- gain_moe: float32 [2048], replicated, may hold values from 0.25 to 1.75
- router: bfloat16 [2048, 64], replicated, may hold values from -0.125 to 0.125
- route_ids: int32 [24576, 8], P(('dp', 'fold', 'tensor')), may hold values from 0 to 63, all different within a row; in each aligned block of 32 rows (0 to 31, 32 to 63, ...) at most 6 rows name the same one
- w_gate: bfloat16 [64, 2048, 768], P(('fold', 'tensor')), may hold values from -0.125 to 0.125
- w_up: bfloat16 [64, 2048, 768], P(('fold', 'tensor')), may hold values from -0.125 to 0.125
- w_down: bfloat16 [64, 768, 2048], P(('fold', 'tensor')), may hold values from -0.21875 to 0.21875
- bias: float32 [64], replicated, may hold values from -1 to 1
- gain_next: float32 [2048], replicated, may hold values from 0.25 to 1.75
- w_query: bfloat16 [2048, 4096], P(None, 'tensor'), may hold values from -0.125 to 0.125
Outputs:
- stream_out: bfloat16 [24576, 2048], P(('dp', 'fold', 'tensor'))
- query: bfloat16 [24576, 4096], P(('dp', 'fold'), 'tensor')
- new_bias: float32 [64], replicated
Inputs may be any that keep to these rules, and one draw needn't show every extreme that they name: `route_ids`: each row names 8 different experts; among the rows of one device no expert is named by more than 6 rows.
All inputs are finite; a program needn't handle non-finite values.
Results may differ from a plain program's by a relative error of at most 0.006.
Values may be sent and summed in bfloat16 or wider, within the bound.
A program may use at most 64 MiB of HBM per device.

v0:
```python
import math

import jax
import jax.numpy as jnp
from jax import lax
from jax.sharding import PartitionSpec as P

TOPK = 8


def rms_scale(values, gain):
    mean_sq = jnp.mean(values * values, axis=-1, keepdims=True)
    return values * lax.rsqrt(mean_sq + 1e-06) * gain


def expert_rows(arrived, w_gate, w_up, w_down):
    shape = arrived.shape
    flat_rows = arrived.reshape(-1, shape[-1])
    gate = jnp.dot(flat_rows, w_gate[0], preferred_element_type=jnp.float32)
    upper = jnp.dot(flat_rows, w_up[0], preferred_element_type=jnp.float32)
    act = (jax.nn.silu(gate) * upper).astype(jnp.bfloat16)
    result = jnp.dot(act, w_down[0], preferred_element_type=jnp.float32).astype(jnp.bfloat16)
    return result.reshape(shape)


def local(
    attn_heads,
    w_out,
    residual,
    gain_moe,
    router,
    route_ids,
    w_gate,
    w_up,
    w_down,
    bias,
    gain_next,
    w_query,
):
    tok = residual.shape[0]
    width = residual.shape[1]
    attn_proj = lax.psum_scatter(
        jnp.dot(attn_heads, w_out, preferred_element_type=jnp.float32),
        "tensor",
        scatter_dimension=0,
        tiled=True,
    )
    stream = residual.astype(jnp.float32) + attn_proj
    normed = rms_scale(stream, gain_moe).astype(jnp.bfloat16)
    logits = jnp.dot(normed, router, preferred_element_type=jnp.float32)
    picked = jnp.take_along_axis(logits, route_ids, axis=1)
    scores = jax.nn.sigmoid(picked)
    weights = (scores / jnp.sum(scores, axis=1, keepdims=True)).astype(jnp.bfloat16)
    n_fold = lax.axis_size("fold")
    n_tensor = lax.axis_size("tensor")
    experts = n_fold * n_tensor
    cap = min(tok, max(2, 3 * tok * TOPK // (2 * experts)))
    hits = jnp.sum(
        (route_ids[:, :, None] == jnp.arange(experts, dtype=jnp.int32)[None, None, :]).astype(
            jnp.int32
        ),
        axis=1,
    )
    before = jnp.cumsum(hits, axis=0) - hits
    slots = jnp.take_along_axis(before, route_ids, axis=1)
    target = route_ids * cap + slots
    match = target[:, :, None] == jnp.arange(experts * cap, dtype=jnp.int32)[None, None, :]
    chosen = jnp.any(match, axis=1).astype(jnp.bfloat16)
    send = lax.dot_general(
        chosen, normed, (((0,), (0,)), ((), ())), preferred_element_type=jnp.float32
    )
    send = send.astype(jnp.bfloat16).reshape(experts, cap, width)
    outputs = expert_rows(
        lax.all_to_all(send, ("fold", "tensor"), split_axis=0, concat_axis=0, tiled=True),
        w_gate,
        w_up,
        w_down,
    )
    back = lax.all_to_all(outputs, ("fold", "tensor"), split_axis=0, concat_axis=0, tiled=True)
    back_flat = back.reshape(experts * cap, width)
    mixing = jnp.sum(jnp.where(match, weights[:, :, None], jnp.zeros((), jnp.bfloat16)), axis=1)
    combined = jnp.dot(mixing, back_flat, preferred_element_type=jnp.float32)
    new_stream = stream + combined
    stream_out = new_stream.astype(jnp.bfloat16)
    normed_next = rms_scale(new_stream, gain_next).astype(jnp.bfloat16)
    query = jnp.dot(
        lax.all_gather(normed_next, "tensor", axis=0, tiled=True),
        w_query,
        preferred_element_type=jnp.float32,
    ).astype(jnp.bfloat16)
    counts = lax.psum(jnp.sum(hits, axis=0), ("dp", "fold", "tensor"))
    devices = lax.axis_size("dp") * n_fold * n_tensor
    mean_load = tok * devices * TOPK / experts
    new_bias = bias + 0.5 * (mean_load - counts.astype(jnp.float32)) / math.sqrt(mean_load)
    return (stream_out, query, new_bias)


def solution(mesh):
    in_specs = (
        P(("dp", "fold"), "tensor"),
        P("tensor", None),
        P(("dp", "fold", "tensor"), None),
        P(),
        P(),
        P(("dp", "fold", "tensor"), None),
        P(("fold", "tensor"), None, None),
        P(("fold", "tensor"), None, None),
        P(("fold", "tensor"), None, None),
        P(),
        P(),
        P(None, "tensor"),
    )
    out_specs = (P(("dp", "fold", "tensor"), None), P(("dp", "fold"), "tensor"), P())
    return jax.shard_map(local, mesh=mesh, in_specs=in_specs, out_specs=out_specs, check_vma=False)
```

profile of v0, /device:TPU:1, one launch (start us, length us, event | category | flops | bytes accessed | tf_op | source)
XLA Modules:
  0.0 357.2 jit_solution(3094468624550791512)
XLA Ops:
  7.2 0.0 copy-start
  7.2 0.0 reduce-scatter.2.cloned.1.call-start
  7.2 4.1 %fusion.22 = f32[512,2048]{1,0:T(8,128)} fusion(bf16[512,256]{1,0:T(8,128)(2,1)} %param.12, bf16[256,2048]{1,0:T(8,128)(2,1)} %param.13), kind=kOutput, calls=%fused_computation.38 | convolution fusion | flops 536870912 | bytes 5505024 | tf_op jit(solution)/shard_map/dot_general | solution.py:43
  11.4 0.0 copy-start.3
  11.4 0.0 reduce-scatter.2.cloned.1.call-update
  11.4 0.7 copy-done.3
  12.0 0.1 copy.28
  12.1 0.1 copy.29
  12.2 0.1 reshape.70
  12.3 0.1 convert_reduce_fusion
  12.4 0.1 reduce_window_sum.11
  12.5 0.0 copy-start.2
  12.5 0.0 copy-start.4
  12.5 1.9 gather_fusion
  14.5 0.1 reshape.73
  14.5 0.1 copy.30
  14.6 0.1 copy.31
  14.7 0.2 fusion.18
  14.9 70.8 %reduce-scatter.2.cloned.1.call-done = f32[32,2048]{1,0:T(8,128)} async-done(((f32[512,2048]{1,0:T(8,128)}), f32[32,2048]{1,0:T(8,128)}) %reduce-scatter.2.cloned.1.call-update) | async-done | bytes 262160 | tf_op jit(solution)/shard_map/reduce_scatter | solution.py:42
  85.7 0.0 copy-done.2
  85.7 1.1 multiply_reduce_fusion.1
  86.8 0.0 copy-done.4
  86.8 1.0 multiply_convert_fusion.1
  87.8 1.8 convolution_convert_fusion
  89.6 3.7 %reshape.66 = bf16[64,6,2048]{2,1,0:T(8,128)(2,1)} reshape(bf16[384,2048]{1,0:T(8,128)(2,1)} %convolution_convert_fusion) | data formatting | bytes 3145728 | tf_op jit(solution)/shard_map/reshape | solution.py:72
  93.3 60.7 %all_to_all.10 = bf16[64,6,2048]{2,1,0:T(8,128)(2,1)} all-to-all(bf16[64,6,2048]{2,1,0:T(8,128)(2,1)} %reshape.66), channel_id=1, replica_groups=mesh['dp'=12,'fold'=4,'tensor'=16] {'fold','tensor'}, dimensions={0} | all-to-all | bytes 3145728 | tf_op jit(solution)/shard_map/all_to_all | solution.py:74
  154.0 3.7 %reshape.67 = bf16[384,2048]{1,0:T(8,128)(2,1)} reshape(bf16[64,6,2048]{2,1,0:T(8,128)(2,1)} %all_to_all.10) | data formatting | bytes 3145728 | tf_op jit(solution)/shard_map/reshape | solution.py:18
  157.7 4.8 %fusion.4 = f32[384,768]{1,0:T(8,128)} fusion(bf16[384,2048]{1,0:T(8,128)(2,1)} %reshape.67, bf16[1,2048,768]{2,1,0:T(8,128)(2,1)} %param.18), kind=kOutput, calls=%fused_computation.6 | convolution fusion | flops 1207959552 | bytes 5898240 | tf_op jit(solution)/shard_map/dot_general | solution.py:19
  162.5 0.0 copy-done
  162.5 6.9 %fusion.6 = bf16[384,2048]{1,0:T(8,128)(2,1)} fusion(bf16[1,768,2048]{2,1,0:T(8,128)(2,1)S(1)} %copy-done, bf16[384,2048]{1,0:T(8,128)(2,1)} %reshape.67, bf16[1,2048,768]{2,1,0:T(8,128)(2,1)} %param.19, f32[384,768]{1,0:T(8,128)} %fusion.4), kind=kOutput, calls=%fused_computation.8 | convolution fusion | flops 2418475008 | bytes 10616832 | tf_op jit(solution)/shard_map/dot_general | solution.py:22
  169.3 3.7 %reshape.68 = bf16[64,6,2048]{2,1,0:T(8,128)(2,1)} reshape(bf16[384,2048]{1,0:T(8,128)(2,1)} %fusion.6) | data formatting | bytes 3145728 | tf_op jit(solution)/shard_map/reshape | solution.py:23
  173.0 6.0 %all-to-all-start.1 = ((bf16[64,6,2048]{2,1,0:T(8,128)(2,1)}), bf16[64,6,2048]{2,1,0:T(8,128)(2,1)}, u32[]{:S(2)}, u32[]{:S(2)}) async-start(bf16[64,6,2048]{2,1,0:T(8,128)(2,1)} %reshape.68), calls=%async_computation.2 | async-start | bytes 4194304 | tf_op jit(solution)/shard_map/all_to_all | solution.py:79
  179.0 0.0 all-gather.2.cloned.1.call-start
  179.1 1.1 fusion.23
  180.2 2.0 gather_fusion.1
  182.2 0.1 reshape.79
  182.2 0.1 copy.32
  182.4 0.1 copy.33
  182.5 0.8 fusion.20
  183.3 0.0 copy-start.1
  183.3 46.9 %all-to-all-done.1 = bf16[64,6,2048]{2,1,0:T(8,128)(2,1)} async-done(((bf16[64,6,2048]{2,1,0:T(8,128)(2,1)}), bf16[64,6,2048]{2,1,0:T(8,128)(2,1)}, u32[]{:S(2)}, u32[]{:S(2)}) %all-to-all-start.1) | async-done | bytes 1572896 | tf_op jit(solution)/shard_map/all_to_all | solution.py:79
  230.2 3.7 %reshape.69 = bf16[384,2048]{1,0:T(8,128)(2,1)} reshape(bf16[64,6,2048]{2,1,0:T(8,128)(2,1)} %all-to-all-done.1) | data formatting | bytes 3145728 | tf_op jit(solution)/shard_map/reshape | solution.py:80
  233.9 0.0 copy-done.1
  233.9 0.0 copy-start.5
  233.9 0.0 copy-start.6
  233.9 1.9 multiply_reduce_fusion
  235.8 0.0 copy-done.5
  235.8 0.8 multiply_convert_fusion
  236.6 0.0 all-gather.2.cloned.1.call-update
  236.6 110.0 %psum.7 = s32[64]{0:T(128)S(1)} all-reduce(s32[64]{0:T(128)S(1)} %get-tuple-element.3), channel_id=1, replica_groups=mesh['dp'=12,'fold'=4,'tensor'=16] {'dp','fold','tensor'}, use_global_device_ids=true, to_apply=%region_9.10 | all-reduce | flops 64 | bytes 512 | tf_op jit(solution)/shard_map/psum | solution.py:91
  346.6 0.0 copy-done.6
  346.6 0.5 multiply_add_fusion
  347.1 0.0 all-gather.2.cloned.1.call-done
  347.1 3.3 convolution_convert_fusion.1
  (7 shorter events, 0.1 us)
Async XLA Ops:
  7.2 155.3 %copy-start = (bf16[1,768,2048]{2,1,0:T(8,128)(2,1)S(1)}, bf16[1,768,2048]{2,1,0:T(8,128)(2,1)}, u32[]{:S(2)}) copy-start(bf16[1,768,2048]{2,1,0:T(8,128)(2,1)} %param.20) | copy-start | bytes 9437188
  7.2 78.5 %reduce-scatter.2.cloned.1.call-start = ((), (), s32[]{:S(2)}) async-start(), calls=%async_computation.3 | async-start | bytes 4456448 | tf_op jit(solution)/shard_map/reduce_scatter | solution.py:42
  11.4 0.7 copy-start.3
  12.5 73.2 %copy-start.2 = (bf16[32,2048]{1,0:T(8,128)(2,1)S(1)}, bf16[32,2048]{1,0:T(8,128)(2,1)}, u32[]{:S(2)}) copy-start(bf16[32,2048]{1,0:T(8,128)(2,1)} %param.14) | copy-start | bytes 393220
  12.5 74.3 %copy-start.4 = (f32[2048]{0:T(1024)S(1)}, f32[2048]{0:T(1024)}, u32[]{:S(2)}) copy-start(f32[2048]{0:T(1024)} %param.15) | copy-start | bytes 24580
  173.0 57.2 %all-to-all-start.1 = ((bf16[64,6,2048]{2,1,0:T(8,128)(2,1)}), bf16[64,6,2048]{2,1,0:T(8,128)(2,1)}, u32[]{:S(2)}, u32[]{:S(2)}) async-start(bf16[64,6,2048]{2,1,0:T(8,128)(2,1)} %reshape.68), calls=%async_computation.2 | async-start | bytes 4194304 | tf_op jit(solution)/shard_map/all_to_all | solution.py:79
  179.0 168.1 %all-gather.2.cloned.1.call-start = ((), (), s32[]{:S(2)}) async-start(), calls=%async_computation.4 | async-start | bytes 2228224 | tf_op jit(solution)/shard_map/all_gather | solution.py:87
  183.3 50.6 %copy-start.1 = (f32[32,2048]{1,0:T(8,128)S(1)}, f32[32,2048]{1,0:T(8,128)}, u32[]{:S(2)}) copy-start(f32[32,2048]{1,0:T(8,128)} %reduce-scatter.2.cloned.1.call-done) | copy-start | bytes 786436
  233.9 2.0 copy-start.5
  233.9 112.7 %copy-start.6 = (f32[64]{0:T(128)S(1)}, f32[64]{0:T(128)}, u32[]{:S(2)}) copy-start(f32[64]{0:T(128)} %param.21) | copy-start | bytes 772
Sparse Core Ops, SparseCore 0:
  11.5 74.1 reduce-scatter.1
  236.7 41.8 all-gather.1
where the time goes:
time: 358 us; the launch traced here: 357 us
  blocking collectives  171 us (48%)
  waiting for transfers between devices  118 us (33%)
  matrix products  23.9 us (7%)
  local copies, waits for them, and re-layouts  20.1 us (6%)
  between operations  14.2 us (4%)
  starting transfers between devices  6.08 us (2%)
  other arithmetic  4.72 us (1%)
    psum x1, blocking collectives, local(): counts = lax.psum(jnp.sum(hits, axis=0), ('dp', 'fold', 'tensor'))  110 us
    reduce_scatter x1, waiting for transfers between devices, local(): lax.psum_scatter(jnp.dot(attn_heads, w_out, preferred_element_type=jnp.fl...  70.8 us
    all_to_all x1, blocking collectives, local(): lax.all_to_all(send, ('fold', 'tensor'), split_axis=0, concat_axis=0, til...  60.7 us
    all_to_all x1, waiting for transfers between devices, local(): lax.all_to_all(outputs, ('fold', 'tensor'), split_axis=0, concat_axis=0,...  46.9 us
  transfers between devices with their start and end apart: 3, of which 2 were waited for; matrix products, arithmetic and copies ran while one was open for 2% of the time, Pallas kernels for 0%

commit v1 on v0

v1 whole, which is shorter than its diff:
```python
import math

import jax
import jax.numpy as jnp
from jax import lax
from jax.experimental import pallas as pl
from jax.experimental.pallas import tpu as pltpu
from jax.sharding import PartitionSpec as P

TOK = 32
HALF = 16
CAP = 6
NY = 8
NX = 4
NZ = 12
MEAN_LOAD = 3072.0

REL = (0, -1, 1, -2, 2, -3, 3, 4)
AG_SRC = ((0, 1, 3, 5), (0, 2, 4, 6))
AG_DST = ((1, 3, 5, 7), (2, 4, 6, 7))
RS_BLK = ((7, 6, 4, 2), (7, 5, 3, 1))
TILE_BLOCKS = ((0, 2), (2, 5), (5, 7))

BF = jnp.bfloat16
F32 = jnp.float32


def dot(a, b):
    return jnp.dot(a, b, preferred_element_type=F32)


def kernel(
    attn, w_out, residual, gain1, router_t, ids_t, w_gate, w_up, w_down, bias, gain2, w_query,
    stream_out, query, new_bias,
    attn_v, w_out_v, wg, wu, wd, wq,
    part, sib_send, sib_recv,
    rs1_send, rs1_recv, rs2_send, rs2_recv,
    norm, norm2, stream, comb,
    table, pick, mix,
    x_send, x_recv, y_send, y_recv,
    cx_send, cx_recv, cz_send, cz_recv,
    sem_attn, sem_w, s_sib, r_sib,
    s_rs1, r_rs1, s_rs2, r_rs2, s_ag1, r_ag1, s_ag2, r_ag2, s_agc, r_agc, s_tab, r_tab,
    s_x, r_x, s_y, r_y, s_cx, r_cx, s_cz, r_cz,
):
    z = lax.axis_index("dp")
    x = lax.axis_index("fold")
    t = lax.axis_index("tensor")
    y = t // 2
    c = t % 2
    sib = {"tensor": y * 2 + (1 - c)}
    ring = ({"tensor": (t + 2) % 16}, {"tensor": (t + 14) % 16})

    def plane(dx, cr, sign):
        core = c + cr * (1 - 2 * c)
        return {"fold": (x + sign * dx + NX) % NX, "tensor": y * 2 + core}

    pending = []

    def send(src, dst, ss, rs, dev):
        copy = pltpu.make_async_remote_copy(
            src_ref=src, dst_ref=dst, send_sem=ss, recv_sem=rs,
            device_id=dev, device_id_type=pl.DeviceIdType.MESH,
        )
        copy.start()
        pending.append(copy)
        return copy

    attn_copies = []
    for par in range(2):
        for a in range(8):
            core = c if par == 1 else 1 - c
            row = ((y + REL[a] + NY) % NY * 2 + core) * TOK
            copy = pltpu.make_async_copy(
                attn.at[pl.ds(pl.multiple_of(row, TOK), TOK), :],
                attn_v.at[pl.ds((par * 8 + a) * TOK, TOK), :],
                sem_attn.at[par * 8 + a],
            )
            copy.start()
            attn_copies.append(copy)
    w_copies = []
    for i, (src, dst) in enumerate(
        ((w_out, w_out_v), (w_gate.at[0], wg), (w_up.at[0], wu), (w_down.at[0], wd), (w_query, wq))
    ):
        copy = pltpu.make_async_copy(src, dst, sem_w.at[i])
        copy.start()
        w_copies.append(copy)

    barrier = pltpu.get_barrier_semaphore()
    peers = [ring[0], ring[1], sib]
    for dx in range(1, NX):
        for cr in range(2):
            peers.append(plane(dx, cr, 1))
    for dz in range(1, NZ):
        peers.append({"dp": (z + dz) % NZ})
    for peer in peers:
        pl.semaphore_signal(barrier, inc=1, device_id=peer, device_id_type=pl.DeviceIdType.MESH)
    pl.semaphore_wait(barrier, len(peers))

    expert = lax.broadcasted_iota(jnp.int32, (128, TOK), 0)
    hit = jnp.zeros((128, TOK), F32)
    for k in range(8):
        hit = hit + jnp.where(expert == ids_t[k : k + 1, :], 1.0, 0.0)
    rows = lax.broadcasted_iota(jnp.int32, (TOK, TOK), 0)
    cols = lax.broadcasted_iota(jnp.int32, (TOK, TOK), 1)
    before = dot(hit.astype(BF), jnp.where(rows < cols, 1.0, 0.0).astype(BF))
    slot = jnp.where(hit > 0.5, before, -1.0).astype(BF)
    eye = jnp.where(rows == cols, 1.0, 0.0).astype(BF)
    own_table = lax.dot_general(eye, slot, (((1,), (1,)), ((), ())), preferred_element_type=F32)
    table[0:TOK, :] = own_table.astype(BF)

    def table_send(d, s):
        return send(
            table.at[pl.ds(AG_SRC[d][s] * TOK, TOK), :],
            table.at[pl.ds(AG_DST[d][s] * TOK, TOK), :],
            s_tab.at[d * 4 + s], r_tab.at[d * 4 + s], ring[d],
        )

    tab = {}
    for d in range(2):
        tab[d, 0] = table_send(d, 0)

    w_copies[0].wait()
    for a in range(8):
        attn_copies[a].wait()
    sib_copies = []
    for piece in (1, 0):
        lo = piece * 128
        for col in range(0, 2048, 512):
            sib_send[lo : lo + 128, col : col + 512] = dot(
                attn_v[lo : lo + 128, :], w_out_v[:, col : col + 512]
            ).astype(BF)
        sib_copies.append(
            send(
                sib_send.at[pl.ds(lo, 128), :], sib_recv.at[pl.ds(lo, 128), :],
                s_sib.at[piece], r_sib.at[piece], sib,
            )
        )
    for a in range(8):
        attn_copies[8 + a].wait()
    for col in range(0, 2048, 512):
        part[:, col : col + 512] = dot(attn_v[256:512, :], w_out_v[:, col : col + 512])

    def rs_step(s, own, send_buf, recv_buf, ss, rs, copies):
        for h in range(2):
            for d in range(2):
                if s == 0 and h != d:
                    continue
                idx = d * 8 + s * 2 + h
                value = own(RS_BLK[d][s], h)
                if (d, s - 1, h) in copies:
                    copies[d, s - 1, h].wait_recv()
                    prev = (idx - 2) * HALF
                    value = value + recv_buf[prev : prev + HALF, :].astype(F32)
                here = pl.ds(idx * HALF, HALF)
                send_buf[idx * HALF : (idx + 1) * HALF, :] = value.astype(BF)
                copies[d, s, h] = send(
                    send_buf.at[here, :], recv_buf.at[here, :], ss.at[idx], rs.at[idx], ring[d]
                )

    def rs_last(h, own, recv_buf, copies):
        value = own(0, h)
        for d in range(2):
            copies[d, 3, h].wait_recv()
            at = (d * 8 + 6 + h) * HALF
            value = value + recv_buf[at : at + HALF, :].astype(F32)
        return value

    def own1(a, h):
        at = a * TOK + h * HALF
        return part[at : at + HALF, :] + sib_recv[at : at + HALF, :].astype(F32)

    rs1 = {}
    sib_copies[0].wait_recv()
    for s in range(2):
        rs_step(s, own1, rs1_send, rs1_recv, s_rs1, r_rs1, rs1)
        for d in range(2):
            tab[d, s].wait_recv()
            tab[d, s + 1] = table_send(d, s + 1)
    sib_copies[1].wait_recv()
    rs_step(2, own1, rs1_send, rs1_recv, s_rs1, r_rs1, rs1)
    for d in range(2):
        tab[d, 2].wait_recv()
    tab[0, 3] = table_send(0, 3)
    rs_step(3, own1, rs1_send, rs1_recv, s_rs1, r_rs1, rs1)
    tab[0, 3].wait_recv()

    all_slots = table[...].astype(F32)
    count = jnp.sum(jnp.where(all_slots > -0.5, 1.0, 0.0), axis=0, keepdims=True)
    cx_send[...] = jnp.broadcast_to(count, (8, 128))
    cx = []
    for dest in range(1, 8):
        cx.append(
            send(
                cx_send, cx_recv.at[pl.ds(dest * 8, 8), :],
                s_cx.at[dest], r_cx.at[dest], plane(dest // 2, dest % 2, 1),
            )
        )

    e_at = lax.broadcasted_iota(jnp.int32, (128, 384), 0)
    r_at = lax.broadcasted_iota(jnp.int32, (128, 384), 1)
    dest_at = (r_at >> 4) & 7
    cr_at = dest_at & 1
    e_of = ((x + (dest_at >> 1)) & 3) * 16 + y * 2 + c + cr_at * (1 - 2 * c)
    select = jnp.where(e_at == e_of, 1.0, 0.0).astype(BF)
    r_row = lax.broadcasted_iota(jnp.int32, (256, 384), 1)
    packed = (r_row >> 7) * 16 + (r_row & 15)
    block_of = (packed * 43) >> 8
    slot_of = (packed - block_of * 6).astype(F32)
    tok_block = lax.broadcasted_iota(jnp.int32, (256, 384), 0) >> 5
    spread = dot(table[...], select)
    match = jnp.logical_and(spread == slot_of, tok_block == block_of)
    pick[...] = jnp.where(match, 1.0, 0.0)

    def normalize(value, gain):
        mean_sq = jnp.mean(value * value, axis=-1, keepdims=True)
        return (value * lax.rsqrt(mean_sq + 1e-06) * gain[...]).astype(BF)

    def ag_send(buf, scale, d, s, h, ss, rs):
        src = AG_SRC[d][s] * scale + h * HALF
        dst = AG_DST[d][s] * scale + h * HALF
        idx = d * 8 + s * 2 + h
        return send(
            buf.at[pl.ds(src, HALF), :], buf.at[pl.ds(dst, HALF), :], ss.at[idx], rs.at[idx], ring[d]
        )

    ag1 = {}
    for h in range(2):
        at = h * HALF
        value = residual[at : at + HALF, :].astype(F32) + rs_last(h, own1, rs1_recv, rs1)
        stream[at : at + HALF, :] = value
        norm[at : at + HALF, :] = normalize(value, gain1)
        for d in range(2):
            ag1[d, 0, h] = ag_send(norm, TOK, d, 0, h, s_ag1, r_ag1)

    def ag1_pass(s):
        for h in range(2):
            for d in range(2):
                if (d, s, h) not in ag1:
                    continue
                ag1[d, s, h].wait_recv()
                if s < 2 or (s == 2 and h == d):
                    ag1[d, s + 1, h] = ag_send(norm, TOK, d, s + 1, h, s_ag1, r_ag1)

    xs = {}

    def dispatch(g):
        lo, hi = TILE_BLOCKS[g][0] * TOK, (TILE_BLOCKS[g][1] + 1) * TOK
        lhs = pick[lo:hi, g * 128 : (g + 1) * 128].T.astype(BF)
        for col in range(0, 2048, 512):
            x_send[g * 128 : (g + 1) * 128, col : col + 512] = dot(
                lhs, norm[lo:hi, col : col + 512]
            ).astype(BF)
        for dest in (4, 5, 2, 3, 6, 7, 1):
            at = pl.ds(g * 128 + dest * HALF, HALF)
            xs[g, dest] = send(
                x_send.at[at, :], x_recv.at[at, :],
                s_x.at[g * 8 + dest], r_x.at[g * 8 + dest], plane(dest // 2, dest % 2, 1),
            )
        x_recv[g * 128 : g * 128 + HALF, :] = x_send[g * 128 : g * 128 + HALF, :]

    ag1_pass(0)
    dispatch(0)
    ag1_pass(1)
    ag1_pass(2)
    dispatch(1)
    ag1_pass(3)
    dispatch(2)

    logits = lax.dot_general(
        norm[...], router_t[...], (((1,), (1,)), ((), ())), preferred_element_type=F32
    )
    score = 1.0 / (1.0 + jnp.exp(-logits))
    score = jnp.where(table[:, 0:64].astype(F32) > -0.5, score, 0.0)
    weight = (score / jnp.sum(score, axis=1, keepdims=True)).astype(BF)
    mix[...] = (dot(weight, select[0:64, :]) * pick[...]).astype(BF)

    total = cx_send[...]
    for dest in range(1, 8):
        cx[dest - 1].wait_recv()
        total = total + cx_recv[dest * 8 : dest * 8 + 8, :]
    cz_send[...] = total
    cz = []
    for dz in range(1, NZ):
        cz.append(
            send(
                cz_send, cz_recv.at[pl.ds(dz * 8, 8), :],
                s_cz.at[dz], r_cz.at[dz], {"dp": (z + dz) % NZ},
            )
        )

    w_copies[1].wait()
    w_copies[2].wait()
    w_copies[3].wait()
    for g in range(3):
        for dest in (2, 3, 6, 7, 4, 5, 1):
            xs[g, dest].wait_recv()
        arrived = x_recv[g * 128 : (g + 1) * 128, :]
        gate = dot(arrived, wg[...])
        upper = dot(arrived, wu[...])
        act = (gate / (1.0 + jnp.exp(-gate)) * upper).astype(BF)
        for col in range(0, 2048, 512):
            y_send[g * 128 : (g + 1) * 128, col : col + 512] = dot(
                act, wd[:, col : col + 512]
            ).astype(BF)

    ys = {}
    for g in (2, 1, 0):
        for dest in (4, 5, 2, 3, 6, 7, 1):
            at = pl.ds(g * 128 + dest * HALF, HALF)
            ys[g, dest] = send(
                y_send.at[at, :], y_recv.at[at, :],
                s_y.at[g * 8 + dest], r_y.at[g * 8 + dest], plane(dest // 2, dest % 2, -1),
            )
        y_recv[g * 128 : g * 128 + HALF, :] = y_send[g * 128 : g * 128 + HALF, :]

    def own2(a, h):
        at = a * TOK + h * HALF
        return comb[at : at + HALF, :]

    def mixdown(g):
        for dest in (2, 3, 6, 7, 4, 5, 1):
            ys[g, dest].wait_recv()
        lo, hi = TILE_BLOCKS[g][0] * TOK, (TILE_BLOCKS[g][1] + 1) * TOK
        for col in range(0, 2048, 512):
            value = dot(
                mix[lo:hi, g * 128 : (g + 1) * 128],
                y_recv[g * 128 : (g + 1) * 128, col : col + 512],
            )
            if g == 2:
                comb[lo:hi, col : col + 512] = value
            else:
                comb[lo : hi - TOK, col : col + 512] = value[: hi - TOK - lo, :]
                comb[hi - TOK : hi, col : col + 512] += value[hi - TOK - lo :, :]

    rs2 = {}
    mixdown(2)
    rs_step(0, own2, rs2_send, rs2_recv, s_rs2, r_rs2, rs2)
    mixdown(1)
    rs_step(1, own2, rs2_send, rs2_recv, s_rs2, r_rs2, rs2)
    rs_step(2, own2, rs2_send, rs2_recv, s_rs2, r_rs2, rs2)
    mixdown(0)
    rs_step(3, own2, rs2_send, rs2_recv, s_rs2, r_rs2, rs2)

    total = cz_send[...]
    for dz in range(1, NZ):
        cz[dz - 1].wait_recv()
        total = total + cz_recv[dz * 8 : dz * 8 + 8, :]
    new_bias[...] = bias[...] + 0.5 * (MEAN_LOAD - total[0:1, 0:64]) / math.sqrt(MEAN_LOAD)

    ag2 = {}
    agc = {}

    def share(a, h):
        src = pl.ds(a * 2 * TOK + h * HALF, HALF)
        dst = pl.ds((a * 2 + 1) * TOK + h * HALF, HALF)
        agc[a, h] = send(
            norm2.at[src, :], norm2.at[dst, :], s_agc.at[a * 2 + h], r_agc.at[a * 2 + h], sib
        )

    for h in range(2):
        at = h * HALF
        value = stream[at : at + HALF, :] + rs_last(h, own2, rs2_recv, rs2)
        stream_out[at : at + HALF, :] = value.astype(BF)
        norm2[at : at + HALF, :] = normalize(value, gain2)
        for d in range(2):
            ag2[d, 0, h] = ag_send(norm2, 2 * TOK, d, 0, h, s_ag2, r_ag2)
        share(0, h)

    def ag2_pass(s):
        for h in range(2):
            for d in range(2):
                if (d, s, h) not in ag2:
                    continue
                ag2[d, s, h].wait_recv()
                if s < 2 or (s == 2 and h == d):
                    ag2[d, s + 1, h] = ag_send(norm2, 2 * TOK, d, s + 1, h, s_ag2, r_ag2)
                share(AG_DST[d][s], h)

    def project(first, last):
        for a in range(first, last + 1):
            for h in range(2):
                agc[a, h].wait_recv()
        lo, hi = first * 2 * TOK, (last + 1) * 2 * TOK
        value = dot(norm2[lo:hi, :], wq[...]).astype(BF)
        for a in range(first, last + 1):
            for par in range(2):
                core = c if par == 0 else 1 - c
                row = ((y + REL[a] + NY) % NY * 2 + core) * TOK
                at = ((a - first) * 2 + par) * TOK
                query[pl.ds(pl.multiple_of(row, TOK), TOK), :] = value[at : at + TOK, :]

    w_copies[4].wait()
    ag2_pass(0)
    project(0, 0)
    ag2_pass(1)
    project(1, 2)
    ag2_pass(2)
    project(3, 4)
    ag2_pass(3)
    project(5, 6)
    project(7, 7)

    for copy in pending:
        copy.wait_send()


def local(
    attn_heads, w_out, residual, gain_moe, router, route_ids,
    w_gate, w_up, w_down, bias, gain_next, w_query,
):
    width = residual.shape[1]
    vmem = pl.BlockSpec(memory_space=pltpu.VMEM)
    hbm = pl.BlockSpec(memory_space=pl.ANY)
    dma = pltpu.SemaphoreType.DMA
    scratch = [
        pltpu.VMEM((512, 256), BF), pltpu.VMEM((256, 2048), BF),
        pltpu.VMEM((2048, 768), BF), pltpu.VMEM((2048, 768), BF),
        pltpu.VMEM((768, 2048), BF), pltpu.VMEM((2048, 256), BF),
        pltpu.VMEM((256, width), F32), pltpu.VMEM((256, width), BF), pltpu.VMEM((256, width), BF),
        pltpu.VMEM((256, width), BF), pltpu.VMEM((256, width), BF),
        pltpu.VMEM((256, width), BF), pltpu.VMEM((256, width), BF),
        pltpu.VMEM((256, width), BF), pltpu.VMEM((512, width), BF),
        pltpu.VMEM((TOK, width), F32), pltpu.VMEM((256, width), F32),
        pltpu.VMEM((256, 128), BF), pltpu.VMEM((256, 384), F32), pltpu.VMEM((256, 384), BF),
        pltpu.VMEM((384, width), BF), pltpu.VMEM((384, width), BF),
        pltpu.VMEM((384, width), BF), pltpu.VMEM((384, width), BF),
        pltpu.VMEM((8, 128), F32), pltpu.VMEM((64, 128), F32),
        pltpu.VMEM((8, 128), F32), pltpu.VMEM((96, 128), F32),
        dma((16,)), dma((5,)), dma((2,)), dma((2,)),
        dma((16,)), dma((16,)), dma((16,)), dma((16,)),
        dma((16,)), dma((16,)), dma((16,)), dma((16,)),
        dma((16,)), dma((16,)), dma((8,)), dma((8,)),
        dma((24,)), dma((24,)), dma((24,)), dma((24,)),
        dma((8,)), dma((8,)), dma((12,)), dma((12,)),
    ]
    stream_out, query, new_bias = pl.pallas_call(
        kernel,
        out_shape=(
            jax.ShapeDtypeStruct((TOK, width), BF),
            jax.ShapeDtypeStruct((512, 256), BF),
            jax.ShapeDtypeStruct((1, 64), F32),
        ),
        in_specs=[hbm, hbm, vmem, vmem, vmem, vmem, hbm, hbm, hbm, vmem, vmem, hbm],
        out_specs=(vmem, vmem, vmem),
        scratch_shapes=scratch,
        compiler_params=pltpu.CompilerParams(
            collective_id=0, has_side_effects=True, vmem_limit_bytes=52 * 1024 * 1024
        ),
    )(
        attn_heads, w_out, residual, gain_moe.reshape(1, -1), router.T, route_ids.T,
        w_gate, w_up, w_down, bias.reshape(1, -1), gain_next.reshape(1, -1), w_query,
    )
    return stream_out, query, new_bias.reshape(-1)


def solution(mesh):
    in_specs = (
        P(("dp", "fold"), "tensor"),
        P("tensor", None),
        P(("dp", "fold", "tensor"), None),
        P(),
        P(),
        P(("dp", "fold", "tensor"), None),
        P(("fold", "tensor"), None, None),
        P(("fold", "tensor"), None, None),
        P(("fold", "tensor"), None, None),
        P(),
        P(),
        P(None, "tensor"),
    )
    out_specs = (P(("dp", "fold", "tensor"), None), P(("dp", "fold"), "tensor"), P())
    return jax.shard_map(local, mesh=mesh, in_specs=in_specs, out_specs=out_specs, check_vma=False)
```

time: 358 us -> 117 us (0.33)
  blocking collectives: 171 us -> 0 us
  waiting for transfers between devices: 118 us -> 0 us
  Pallas kernels: 0 us -> 109 us
  matrix products: 23.9 us -> 0 us
  between operations: 14.2 us -> 0.66 us
  local copies, waits for them, and re-layouts: 20.1 us -> 7.4 us
  starting transfers between devices: 6.08 us -> 0 us
  other arithmetic: 4.72 us -> 0 us
    psum x1 -> x0, blocking collectives: 110 us -> none  [local(): counts = lax.psum(jnp.sum(hits, axis=0), ('dp', 'fold', 'tensor'))]
    pallas_call x0 -> x1, Pallas kernels: none -> 109 us  [local(): pl.pallas_call(kernel, out_shape=(jax.ShapeDtypeStruct((TOK, width), BF),...]
    reduce_scatter x1 -> x0, waiting for transfers between devices: 70.8 us -> none  [local(): lax.psum_scatter(jnp.dot(attn_heads, w_out, preferred_element_type=jnp.fl...]
    all_to_all x1 -> x0, blocking collectives: 60.7 us -> none  [local(): lax.all_to_all(send, ('fold', 'tensor'), split_axis=0, concat_axis=0, til...]
    all_to_all x1 -> x0, waiting for transfers between devices: 46.9 us -> none  [local(): lax.all_to_all(outputs, ('fold', 'tensor'), split_axis=0, concat_axis=0,...]
    dot_general x7 -> x0, matrix products: 23.9 us -> none  [the longest x1 6.86 us: expert_rows(): jnp.dot(act, w_down[0], preferred_element_type=jnp.float32)]
    reshape x4 -> x0, local copies, waits for them, and re-layouts: 14.8 us -> none  [the longest x1 3.74 us: expert_rows(): flat_rows = arrived.reshape(-1, shape[-1])]
    unnamed x15 -> x17, local copies, waits for them, and re-layouts: 0.77 us -> 7.4 us
  transfers between devices with their start and end apart: 3 -> 0, of which waited for: 2 -> 0; matrix products, arithmetic and copies ran while one was open for 2% -> 0% of each run, Pallas kernels for 0% -> 0%
where the time goes in v1:
time: 117 us
  Pallas kernels  109 us (93%)
  local copies, waits for them, and re-layouts  7.4 us (6%)
    pallas_call x1, Pallas kernels, local(): pl.pallas_call(kernel, out_shape=(jax.ShapeDtypeStruct((TOK, width), BF),...  109 us
    unnamed x17, local copies, waits for them, and re-layouts  7.4 us

profile of v1, /device:TPU:1, one launch (start us, length us, event | category | flops | bytes accessed | tf_op | source)
XLA Modules:
  0.0 116.8 jit_solution(10483167072223906589)
XLA Ops:
  0.6 0.0 copy-start
  0.6 0.9 copy-done
  1.6 0.0 copy-start.1
  1.6 0.9 copy-done.1
  2.5 0.0 copy-start.2
  2.5 0.9 copy-done.2
  3.4 0.0 copy-start.3
  3.4 0.7 copy-done.3
  4.1 0.0 copy-start.4
  4.1 0.7 copy-done.4
  4.8 0.0 copy-start.5
  4.8 0.7 copy-done.5
  5.5 0.0 copy-start.6
  5.5 0.7 copy-done.6
  6.2 108.7 %shard_map.139 = (bf16[32,2048]{1,0:T(8,128)(2,1)S(1)}, bf16[512,256]{1,0:T(8,128)(2,1)S(1)}, f32[1,64]{1,0:T(1,128)S(1)}) custom-call(bf16[512,256]{1,0:T(8,128)(2,1)S(1)} %copy-done, bf16[256,2048]{1,0:T(8,128)(2,1)} %w_out.1, bf16[32,2048]{1,0:T(8,128)(2,1)S(1)} %copy-done.2, f32[1,2048]{1,0:T(1,128)S(1)} %bitcast.7, bf16[64,2048]{1,0:T(8,128)(2,1)S(1)} %bitcast.6, ...), custom_call_target="tpu_custom_call" | custom-call | tf_op jit(solution)/shard_map/pallas_call | solution.py:437
  114.9 0.7 copy.18
  115.6 0.7 copy.19
  116.3 0.5 copy.20
Async XLA Ops:
  0.6 1.0 copy-start
  1.6 0.9 copy-start.1
  2.5 0.9 copy-start.2
  3.4 0.7 copy-start.3
  4.1 0.7 copy-start.4
  4.8 0.7 copy-start.5
  5.5 0.7 copy-start.6

commit v2 on v1

--- a/solution.py
+++ b/solution.py
@@ -30,16 +30,17 @@
 
 
 def kernel(
-    attn, w_out, residual, gain1, router_t, ids_t, w_gate, w_up, w_down, bias, gain2, w_query,
+    attn, w_out, residual_h, gain1_h, router_h, ids_h, w_gate, w_up, w_down, bias_h, gain2_h, w_query,
     stream_out, query, new_bias,
-    attn_v, w_out_v, wg, wu, wd, wq,
+    attn_v, attn_o, w_out_v, wg, wu, wd, wq,
+    residual, gain1, router_t, ids_t, bias, gain2,
     part, sib_send, sib_recv,
     rs1_send, rs1_recv, rs2_send, rs2_recv,
     norm, norm2, stream, comb,
-    table, pick, mix,
+    table, pick, pick_t, mix,
     x_send, x_recv, y_send, y_recv,
-    cx_send, cx_recv, cz_send, cz_recv,
-    sem_attn, sem_w, s_sib, r_sib,
+    cx_send, cx_recv, cz,
+    sem_load, s_sib, r_sib,
     s_rs1, r_rs1, s_rs2, r_rs2, s_ag1, r_ag1, s_ag2, r_ag2, s_agc, r_agc, s_tab, r_tab,
     s_x, r_x, s_y, r_y, s_cx, r_cx, s_cz, r_cz,
 ):
@@ -66,37 +67,34 @@
         pending.append(copy)
         return copy
 
-    attn_copies = []
-    for par in range(2):
-        for a in range(8):
-            core = c if par == 1 else 1 - c
-            row = ((y + REL[a] + NY) % NY * 2 + core) * TOK
-            copy = pltpu.make_async_copy(
-                attn.at[pl.ds(pl.multiple_of(row, TOK), TOK), :],
-                attn_v.at[pl.ds((par * 8 + a) * TOK, TOK), :],
-                sem_attn.at[par * 8 + a],
-            )
-            copy.start()
-            attn_copies.append(copy)
-    w_copies = []
-    for i, (src, dst) in enumerate(
-        ((w_out, w_out_v), (w_gate.at[0], wg), (w_up.at[0], wu), (w_down.at[0], wd), (w_query, wq))
-    ):
-        copy = pltpu.make_async_copy(src, dst, sem_w.at[i])
-        copy.start()
-        w_copies.append(copy)
-
     barrier = pltpu.get_barrier_semaphore()
-    peers = [ring[0], ring[1], sib]
+    peers = [sib, ring[0], ring[1]]
     for dx in range(1, NX):
         for cr in range(2):
             peers.append(plane(dx, cr, 1))
-    for dz in range(1, NZ):
-        peers.append({"dp": (z + dz) % NZ})
     for peer in peers:
         pl.semaphore_signal(barrier, inc=1, device_id=peer, device_id_type=pl.DeviceIdType.MESH)
-    pl.semaphore_wait(barrier, len(peers))
-
+    for k in range(1, NZ):
+
+        @pl.when(z + k < NZ)
+        def _(k=k):
+            pl.semaphore_signal(
+                barrier, inc=1, device_id={"dp": (z + k) % NZ}, device_id_type=pl.DeviceIdType.MESH
+            )
+
+    def load(i, src, dst):
+        copy = pltpu.make_async_copy(src, dst, sem_load.at[i])
+        copy.start()
+        return copy
+
+    load_ids = load(0, ids_h, ids_t)
+    load_attn = load(1, attn, attn_v)
+    load_w_out = load(2, w_out, w_out_v)
+    load_residual = load(3, residual_h, residual)
+    load_gain1 = load(4, gain1_h, gain1)
+    load_router = load(5, router_h, router_t)
+
+    load_ids.wait()
     expert = lax.broadcasted_iota(jnp.int32, (128, TOK), 0)
     hit = jnp.zeros((128, TOK), F32)
     for k in range(8):
@@ -116,47 +114,56 @@
             s_tab.at[d * 4 + s], r_tab.at[d * 4 + s], ring[d],
         )
 
+    load_attn.wait()
+    for par in range(2):
+        for a in range(8):
+            core = c if par == 1 else 1 - c
+            row = ((y + REL[a] + NY) % NY * 2 + core) * TOK
+            at = (par * 8 + a) * TOK
+            attn_o[at : at + TOK, :] = attn_v[pl.ds(pl.multiple_of(row, TOK), TOK), :]
+    load_w_out.wait()
     tab = {}
-    for d in range(2):
-        tab[d, 0] = table_send(d, 0)
-
-    w_copies[0].wait()
-    for a in range(8):
-        attn_copies[a].wait()
-    sib_copies = []
-    for piece in (1, 0):
-        lo = piece * 128
+    sib_copies = {}
+    for lo in (128, 0):
         for col in range(0, 2048, 512):
             sib_send[lo : lo + 128, col : col + 512] = dot(
-                attn_v[lo : lo + 128, :], w_out_v[:, col : col + 512]
+                attn_o[lo : lo + 128, :], w_out_v[:, col : col + 512]
             ).astype(BF)
-        sib_copies.append(
-            send(
-                sib_send.at[pl.ds(lo, 128), :], sib_recv.at[pl.ds(lo, 128), :],
-                s_sib.at[piece], r_sib.at[piece], sib,
-            )
-        )
-    for a in range(8):
-        attn_copies[8 + a].wait()
-    for col in range(0, 2048, 512):
-        part[:, col : col + 512] = dot(attn_v[256:512, :], w_out_v[:, col : col + 512])
+        if lo == 128:
+            pl.semaphore_wait(barrier, len(peers) + z)
+            for d in range(2):
+                tab[d, 0] = table_send(d, 0)
+        for a in range(lo // TOK + 3, lo // TOK - 1, -1):
+            here = pl.ds(a * TOK, TOK)
+            sib_copies[a] = send(
+                sib_send.at[here, :], sib_recv.at[here, :], s_sib.at[a], r_sib.at[a], sib
+            )
+    for lo in (384, 256):
+        for col in range(0, 2048, 512):
+            part[lo - 256 : lo - 128, col : col + 512] = dot(
+                attn_o[lo : lo + 128, :], w_out_v[:, col : col + 512]
+            )
+    load_wg = load(6, w_gate.at[0], wg)
+    load_wu = load(7, w_up.at[0], wu)
+    load_wd = load(8, w_down.at[0], wd)
+    load_wq = load(9, w_query, wq)
+    load_bias = load(10, bias_h, bias)
+    load_gain2 = load(11, gain2_h, gain2)
 
     def rs_step(s, own, send_buf, recv_buf, ss, rs, copies):
-        for h in range(2):
-            for d in range(2):
-                if s == 0 and h != d:
-                    continue
-                idx = d * 8 + s * 2 + h
-                value = own(RS_BLK[d][s], h)
-                if (d, s - 1, h) in copies:
-                    copies[d, s - 1, h].wait_recv()
-                    prev = (idx - 2) * HALF
-                    value = value + recv_buf[prev : prev + HALF, :].astype(F32)
-                here = pl.ds(idx * HALF, HALF)
-                send_buf[idx * HALF : (idx + 1) * HALF, :] = value.astype(BF)
-                copies[d, s, h] = send(
-                    send_buf.at[here, :], recv_buf.at[here, :], ss.at[idx], rs.at[idx], ring[d]
-                )
+        order = ((0, 0), (1, 1)) if s == 0 else ((0, 1), (1, 0), (0, 0), (1, 1))
+        for d, h in order:
+            idx = d * 8 + s * 2 + h
+            value = own(RS_BLK[d][s], h)
+            if (d, s - 1, h) in copies:
+                copies[d, s - 1, h].wait_recv()
+                prev = (idx - 2) * HALF
+                value = value + recv_buf[prev : prev + HALF, :].astype(F32)
+            here = pl.ds(idx * HALF, HALF)
+            send_buf[idx * HALF : (idx + 1) * HALF, :] = value.astype(BF)
+            copies[d, s, h] = send(
+                send_buf.at[here, :], recv_buf.at[here, :], ss.at[idx], rs.at[idx], ring[d]
+            )
 
     def rs_last(h, own, recv_buf, copies):
         value = own(0, h)
@@ -170,18 +177,23 @@
         at = a * TOK + h * HALF
         return part[at : at + HALF, :] + sib_recv[at : at + HALF, :].astype(F32)
 
+    sib_here = set()
+
+    def sib_wait(*blocks):
+        for a in blocks:
+            if a not in sib_here:
+                sib_here.add(a)
+                sib_copies[a].wait_recv()
+
     rs1 = {}
-    sib_copies[0].wait_recv()
-    for s in range(2):
+    for s in range(3):
+        sib_wait(RS_BLK[0][s], RS_BLK[1][s])
         rs_step(s, own1, rs1_send, rs1_recv, s_rs1, r_rs1, rs1)
         for d in range(2):
             tab[d, s].wait_recv()
-            tab[d, s + 1] = table_send(d, s + 1)
-    sib_copies[1].wait_recv()
-    rs_step(2, own1, rs1_send, rs1_recv, s_rs1, r_rs1, rs1)
-    for d in range(2):
-        tab[d, 2].wait_recv()
-    tab[0, 3] = table_send(0, 3)
+            if s < 2 or d == 0:
+                tab[d, s + 1] = table_send(d, s + 1)
+    sib_wait(2, 1, 0)
     rs_step(3, own1, rs1_send, rs1_recv, s_rs1, r_rs1, rs1)
     tab[0, 3].wait_recv()
 
@@ -211,6 +223,9 @@
     spread = dot(table[...], select)
     match = jnp.logical_and(spread == slot_of, tok_block == block_of)
     pick[...] = jnp.where(match, 1.0, 0.0)
+    pick_t[...] = pick[...].T.astype(BF)
+    load_residual.wait()
+    load_gain1.wait()
 
     def normalize(value, gain):
         mean_sq = jnp.mean(value * value, axis=-1, keepdims=True)
@@ -246,7 +261,7 @@
 
     def dispatch(g):
         lo, hi = TILE_BLOCKS[g][0] * TOK, (TILE_BLOCKS[g][1] + 1) * TOK
-        lhs = pick[lo:hi, g * 128 : (g + 1) * 128].T.astype(BF)
+        lhs = pick_t[g * 128 : (g + 1) * 128, lo:hi]
         for col in range(0, 2048, 512):
             x_send[g * 128 : (g + 1) * 128, col : col + 512] = dot(
                 lhs, norm[lo:hi, col : col + 512]
@@ -259,13 +274,34 @@
             )
         x_recv[g * 128 : g * 128 + HALF, :] = x_send[g * 128 : g * 128 + HALF, :]
 
+    def z_copy(k):
+        return pltpu.make_async_remote_copy(
+            src_ref=cz.at[pl.ds(0, 8), :], dst_ref=cz.at[pl.ds(k * 8, 8), :],
+            send_sem=s_cz.at[k], recv_sem=r_cz.at[k],
+            device_id={"dp": (z + NZ - k) % NZ}, device_id_type=pl.DeviceIdType.MESH,
+        )
+
+    def z_each(cond, act):
+        for k in range(1, NZ):
+
+            @pl.when(cond(k))
+            def _(k=k):
+                act(z_copy(k))
+
     ag1_pass(0)
     dispatch(0)
     ag1_pass(1)
     ag1_pass(2)
     dispatch(1)
+    total = cx_send[...]
+    for dest in range(1, 8):
+        cx[dest - 1].wait_recv()
+        total = total + cx_recv[dest * 8 : dest * 8 + 8, :]
+    cz[0:8, :] = total
+    z_each(lambda k: k <= z, lambda copy: copy.start())
     ag1_pass(3)
     dispatch(2)
+    load_router.wait()
 
     logits = lax.dot_general(
         norm[...], router_t[...], (((1,), (1,)), ((), ())), preferred_element_type=F32
@@ -275,26 +311,24 @@
     weight = (score / jnp.sum(score, axis=1, keepdims=True)).astype(BF)
     mix[...] = (dot(weight, select[0:64, :]) * pick[...]).astype(BF)
 
-    total = cx_send[...]
-    for dest in range(1, 8):
-        cx[dest - 1].wait_recv()
-        total = total + cx_recv[dest * 8 : dest * 8 + 8, :]
-    cz_send[...] = total
-    cz = []
-    for dz in range(1, NZ):
-        cz.append(
-            send(
-                cz_send, cz_recv.at[pl.ds(dz * 8, 8), :],
-                s_cz.at[dz], r_cz.at[dz], {"dp": (z + dz) % NZ},
-            )
-        )
-
-    w_copies[1].wait()
-    w_copies[2].wait()
-    w_copies[3].wait()
+    load_wg.wait()
+    load_wu.wait()
+    load_wd.wait()
+    ys = {}
+
+    def give_back(g, dests):
+        for dest in dests:
+            at = pl.ds(g * 128 + dest * HALF, HALF)
+            ys[g, dest] = send(
+                y_send.at[at, :], y_recv.at[at, :],
+                s_y.at[g * 8 + dest], r_y.at[g * 8 + dest], plane(dest // 2, dest % 2, -1),
+            )
+
     for g in range(3):
         for dest in (2, 3, 6, 7, 4, 5, 1):
             xs[g, dest].wait_recv()
+        if g == 2:
+            give_back(0, (2, 3, 6, 7))
         arrived = x_recv[g * 128 : (g + 1) * 128, :]
         gate = dot(arrived, wg[...])
         upper = dot(arrived, wu[...])
@@ -303,15 +337,14 @@
             y_send[g * 128 : (g + 1) * 128, col : col + 512] = dot(
                 act, wd[:, col : col + 512]
             ).astype(BF)
-
-    ys = {}
-    for g in (2, 1, 0):
-        for dest in (4, 5, 2, 3, 6, 7, 1):
-            at = pl.ds(g * 128 + dest * HALF, HALF)
-            ys[g, dest] = send(
-                y_send.at[at, :], y_recv.at[at, :],
-                s_y.at[g * 8 + dest], r_y.at[g * 8 + dest], plane(dest // 2, dest % 2, -1),
-            )
+        if g == 2:
+            z_each(lambda k: z + k < NZ, lambda copy: copy.wait_recv())
+            z_each(lambda k: k > z, lambda copy: copy.start())
+
+    give_back(2, (4, 5, 2, 3, 6, 7, 1))
+    give_back(1, (4, 5, 2, 3, 6, 7, 1))
+    give_back(0, (4, 5, 1))
+    for g in range(3):
         y_recv[g * 128 : g * 128 + HALF, :] = y_send[g * 128 : g * 128 + HALF, :]
 
     def own2(a, h):
@@ -342,11 +375,13 @@
     mixdown(0)
     rs_step(3, own2, rs2_send, rs2_recv, s_rs2, r_rs2, rs2)
 
-    total = cz_send[...]
+    z_each(lambda k: z + k >= NZ, lambda copy: copy.wait_recv())
+    total = cz[0:1, :]
     for dz in range(1, NZ):
-        cz[dz - 1].wait_recv()
-        total = total + cz_recv[dz * 8 : dz * 8 + 8, :]
-    new_bias[...] = bias[...] + 0.5 * (MEAN_LOAD - total[0:1, 0:64]) / math.sqrt(MEAN_LOAD)
+        total = total + cz[dz * 8 : dz * 8 + 1, :]
+    load_bias.wait()
+    new_bias[...] = bias[...] + 0.5 * (MEAN_LOAD - total[:, 0:64]) / math.sqrt(MEAN_LOAD)
+    load_gain2.wait()
 
     ag2 = {}
     agc = {}
@@ -390,7 +425,7 @@
                 at = ((a - first) * 2 + par) * TOK
                 query[pl.ds(pl.multiple_of(row, TOK), TOK), :] = value[at : at + TOK, :]
 
-    w_copies[4].wait()
+    load_wq.wait()
     ag2_pass(0)
     project(0, 0)
     ag2_pass(1)
@@ -403,6 +438,8 @@
 
     for copy in pending:
         copy.wait_send()
+    for k in range(1, NZ):
+        z_copy(k).wait_send()
 
 
 def local(
@@ -414,20 +451,23 @@
     hbm = pl.BlockSpec(memory_space=pl.ANY)
     dma = pltpu.SemaphoreType.DMA
     scratch = [
-        pltpu.VMEM((512, 256), BF), pltpu.VMEM((256, 2048), BF),
+        pltpu.VMEM((512, 256), BF), pltpu.VMEM((512, 256), BF), pltpu.VMEM((256, 2048), BF),
         pltpu.VMEM((2048, 768), BF), pltpu.VMEM((2048, 768), BF),
         pltpu.VMEM((768, 2048), BF), pltpu.VMEM((2048, 256), BF),
+        pltpu.VMEM((TOK, width), BF), pltpu.VMEM((1, width), F32), pltpu.VMEM((64, width), BF),
+        pltpu.VMEM((8, TOK), jnp.int32), pltpu.VMEM((1, 64), F32), pltpu.VMEM((1, width), F32),
         pltpu.VMEM((256, width), F32), pltpu.VMEM((256, width), BF), pltpu.VMEM((256, width), BF),
         pltpu.VMEM((256, width), BF), pltpu.VMEM((256, width), BF),
         pltpu.VMEM((256, width), BF), pltpu.VMEM((256, width), BF),
         pltpu.VMEM((256, width), BF), pltpu.VMEM((512, width), BF),
         pltpu.VMEM((TOK, width), F32), pltpu.VMEM((256, width), F32),
-        pltpu.VMEM((256, 128), BF), pltpu.VMEM((256, 384), F32), pltpu.VMEM((256, 384), BF),
+        pltpu.VMEM((256, 128), BF), pltpu.VMEM((256, 384), F32), pltpu.VMEM((384, 256), BF),
+        pltpu.VMEM((256, 384), BF),
         pltpu.VMEM((384, width), BF), pltpu.VMEM((384, width), BF),
         pltpu.VMEM((384, width), BF), pltpu.VMEM((384, width), BF),
         pltpu.VMEM((8, 128), F32), pltpu.VMEM((64, 128), F32),
-        pltpu.VMEM((8, 128), F32), pltpu.VMEM((96, 128), F32),
-        dma((16,)), dma((5,)), dma((2,)), dma((2,)),
+        pltpu.VMEM((96, 128), F32),
+        dma((12,)), dma((8,)), dma((8,)),
         dma((16,)), dma((16,)), dma((16,)), dma((16,)),
         dma((16,)), dma((16,)), dma((16,)), dma((16,)),
         dma((16,)), dma((16,)), dma((8,)), dma((8,)),
@@ -441,11 +481,11 @@
             jax.ShapeDtypeStruct((512, 256), BF),
             jax.ShapeDtypeStruct((1, 64), F32),
         ),
-        in_specs=[hbm, hbm, vmem, vmem, vmem, vmem, hbm, hbm, hbm, vmem, vmem, hbm],
+        in_specs=[hbm] * 12,
         out_specs=(vmem, vmem, vmem),
         scratch_shapes=scratch,
         compiler_params=pltpu.CompilerParams(
-            collective_id=0, has_side_effects=True, vmem_limit_bytes=52 * 1024 * 1024
+            collective_id=0, has_side_effects=True, vmem_limit_bytes=60 * 1024 * 1024
         ),
     )(
         attn_heads, w_out, residual, gain_moe.reshape(1, -1), router.T, route_ids.T,

time: 117 us -> 110 us (0.940)
  Pallas kernels: 109 us -> 104 us
  local copies, waits for them, and re-layouts: 7.4 us -> 4.35 us
    pallas_call x1, Pallas kernels: 109 us -> 104 us  [local(): pl.pallas_call(kernel, out_shape=(jax.ShapeDtypeStruct((TOK, width), BF),...]
    unnamed x17 -> x3, local copies, waits for them, and re-layouts: 7.4 us -> 4.35 us
where the time goes in v2:
time: 110 us; the launch traced here: 109 us
  Pallas kernels  104 us (95%)
  local copies, waits for them, and re-layouts  4.35 us (4%)
    pallas_call x1, Pallas kernels, local(): pl.pallas_call(kernel, out_shape=(jax.ShapeDtypeStruct((TOK, width), BF),...  104 us
    unnamed x3, local copies, waits for them, and re-layouts  4.35 us

profile of v2, /device:TPU:1, one launch (start us, length us, event | category | flops | bytes accessed | tf_op | source)
XLA Modules:
  0.0 109.5 jit_solution(14103487950879180795)
XLA Ops:
  0.6 104.5 %shard_map.139 = (bf16[32,2048]{1,0:T(8,128)(2,1)}, bf16[512,256]{1,0:T(8,128)(2,1)}, f32[1,64]{1,0:T(1,128)}) custom-call(bf16[512,256]{1,0:T(8,128)(2,1)} %attn.1, bf16[256,2048]{1,0:T(8,128)(2,1)} %w_out.1, bf16[32,2048]{1,0:T(8,128)(2,1)} %residual_h.1, f32[1,2048]{1,0:T(1,128)} %bitcast.7, bf16[64,2048]{1,0:T(8,128)(2,1)} %bitcast.6, s32[8,32]{1,0:T(8,128)} %bitcast.9, ...), custom_call_target="tpu_custom_call" | custom-call | tf_op jit(solution)/shard_map/pallas_call | solution.py:477
  105.1 1.6 %copy.18 = bf16[32,2048]{1,0:T(8,128)(2,1)} copy(bf16[32,2048]{1,0:T(8,128)(2,1)} %get-tuple-element.12) | data formatting | bytes 262144
  106.7 1.7 %copy.19 = bf16[512,256]{1,0:T(8,128)(2,1)} copy(bf16[512,256]{1,0:T(8,128)(2,1)} %get-tuple-element.13) | data formatting | bytes 524288
  108.4 1.1 %copy.20 = f32[64]{0:T(128)} copy(f32[64]{0:T(128)} %bitcast.11) | data formatting | bytes 512

commit v3 on v2

--- a/solution.py
+++ b/solution.py
@@ -9,6 +9,7 @@
 
 TOK = 32
 HALF = 16
+WIDE = 1024
 CAP = 6
 NY = 8
 NX = 4
@@ -67,6 +68,11 @@
         pending.append(copy)
         return copy
 
+    def drain(count):
+        for copy in pending[:count]:
+            copy.wait_send()
+        del pending[:count]
+
     barrier = pltpu.get_barrier_semaphore()
     peers = [sib, ring[0], ring[1]]
     for dx in range(1, NX):
@@ -124,25 +130,18 @@
     load_w_out.wait()
     tab = {}
     sib_copies = {}
-    for lo in (128, 0):
-        for col in range(0, 2048, 512):
-            sib_send[lo : lo + 128, col : col + 512] = dot(
-                attn_o[lo : lo + 128, :], w_out_v[:, col : col + 512]
-            ).astype(BF)
-        if lo == 128:
-            pl.semaphore_wait(barrier, len(peers) + z)
-            for d in range(2):
-                tab[d, 0] = table_send(d, 0)
-        for a in range(lo // TOK + 3, lo // TOK - 1, -1):
-            here = pl.ds(a * TOK, TOK)
-            sib_copies[a] = send(
-                sib_send.at[here, :], sib_recv.at[here, :], s_sib.at[a], r_sib.at[a], sib
-            )
-    for lo in (384, 256):
-        for col in range(0, 2048, 512):
-            part[lo - 256 : lo - 128, col : col + 512] = dot(
-                attn_o[lo : lo + 128, :], w_out_v[:, col : col + 512]
-            )
+    for col in range(0, 2048, 512):
+        sib_send[:, col : col + 512] = dot(attn_o[0:256, :], w_out_v[:, col : col + 512]).astype(BF)
+    pl.semaphore_wait(barrier, len(peers) + z)
+    for a in range(7, -1, -1):
+        here = pl.ds(a * TOK, TOK)
+        sib_copies[a] = send(
+            sib_send.at[here, :], sib_recv.at[here, :], s_sib.at[a], r_sib.at[a], sib
+        )
+    for d in range(2):
+        tab[d, 0] = table_send(d, 0)
+    for col in range(0, 2048, 512):
+        part[:, col : col + 512] = dot(attn_o[256:512, :], w_out_v[:, col : col + 512])
     load_wg = load(6, w_gate.at[0], wg)
     load_wu = load(7, w_up.at[0], wu)
     load_wd = load(8, w_down.at[0], wd)
@@ -152,30 +151,38 @@
 
     def rs_step(s, own, send_buf, recv_buf, ss, rs, copies):
         order = ((0, 0), (1, 1)) if s == 0 else ((0, 1), (1, 0), (0, 0), (1, 1))
-        for d, h in order:
-            idx = d * 8 + s * 2 + h
-            value = own(RS_BLK[d][s], h)
-            if (d, s - 1, h) in copies:
-                copies[d, s - 1, h].wait_recv()
-                prev = (idx - 2) * HALF
-                value = value + recv_buf[prev : prev + HALF, :].astype(F32)
-            here = pl.ds(idx * HALF, HALF)
-            send_buf[idx * HALF : (idx + 1) * HALF, :] = value.astype(BF)
-            copies[d, s, h] = send(
-                send_buf.at[here, :], recv_buf.at[here, :], ss.at[idx], rs.at[idx], ring[d]
-            )
+        for first in range(0, len(order), 2):
+            for q in range(2):
+                for d, h in order[first : first + 2]:
+                    idx = d * 8 + s * 2 + h
+                    value = own(RS_BLK[d][s], h, q)
+                    if (d, s - 1, h, q) in copies:
+                        copies[d, s - 1, h, q].wait_recv()
+                        prev = (idx - 2) * HALF
+                        value = value + recv_buf[q, prev : prev + HALF, :].astype(F32)
+                    here = pl.ds(idx * HALF, HALF)
+                    send_buf[q, idx * HALF : (idx + 1) * HALF, :] = value.astype(BF)
+                    copies[d, s, h, q] = send(
+                        send_buf.at[q, here, :], recv_buf.at[q, here, :],
+                        ss.at[idx * 2 + q], rs.at[idx * 2 + q], ring[d],
+                    )
 
     def rs_last(h, own, recv_buf, copies):
-        value = own(0, h)
-        for d in range(2):
-            copies[d, 3, h].wait_recv()
-            at = (d * 8 + 6 + h) * HALF
-            value = value + recv_buf[at : at + HALF, :].astype(F32)
-        return value
-
-    def own1(a, h):
-        at = a * TOK + h * HALF
-        return part[at : at + HALF, :] + sib_recv[at : at + HALF, :].astype(F32)
+        values = []
+        for q in range(2):
+            value = own(0, h, q)
+            for d in range(2):
+                copies[d, 3, h, q].wait_recv()
+                at = (d * 8 + 6 + h) * HALF
+                value = value + recv_buf[q, at : at + HALF, :].astype(F32)
+            values.append(value)
+        return jnp.concatenate(values, axis=1)
+
+    def own1(a, h, q):
+        at, col = a * TOK + h * HALF, q * WIDE
+        return part[at : at + HALF, col : col + WIDE] + sib_recv[
+            at : at + HALF, col : col + WIDE
+        ].astype(F32)
 
     sib_here = set()
 
@@ -337,19 +344,20 @@
             y_send[g * 128 : (g + 1) * 128, col : col + 512] = dot(
                 act, wd[:, col : col + 512]
             ).astype(BF)
-        if g == 2:
-            z_each(lambda k: z + k < NZ, lambda copy: copy.wait_recv())
-            z_each(lambda k: k > z, lambda copy: copy.start())
-
+
+    sent = len(pending)
     give_back(2, (4, 5, 2, 3, 6, 7, 1))
     give_back(1, (4, 5, 2, 3, 6, 7, 1))
     give_back(0, (4, 5, 1))
     for g in range(3):
         y_recv[g * 128 : g * 128 + HALF, :] = y_send[g * 128 : g * 128 + HALF, :]
-
-    def own2(a, h):
-        at = a * TOK + h * HALF
-        return comb[at : at + HALF, :]
+    z_each(lambda k: z + k < NZ, lambda copy: copy.wait_recv())
+    z_each(lambda k: k > z, lambda copy: copy.start())
+    drain(sent)
+
+    def own2(a, h, q):
+        at, col = a * TOK + h * HALF, q * WIDE
+        return comb[at : at + HALF, col : col + WIDE]
 
     def mixdown(g):
         for dest in (2, 3, 6, 7, 4, 5, 1):
@@ -382,42 +390,63 @@
     load_bias.wait()
     new_bias[...] = bias[...] + 0.5 * (MEAN_LOAD - total[:, 0:64]) / math.sqrt(MEAN_LOAD)
     load_gain2.wait()
+    for k in range(1, NZ):
+        z_copy(k).wait_send()
 
     ag2 = {}
     agc = {}
 
-    def share(a, h):
+    def ag2_send(d, s, h, q):
+        src = AG_SRC[d][s] * 2 * TOK + h * HALF
+        dst = AG_DST[d][s] * 2 * TOK + h * HALF
+        idx = (d * 8 + s * 2 + h) * 2 + q
+        ag2[d, s, h, q] = send(
+            norm2.at[q, pl.ds(src, HALF), :], norm2.at[q, pl.ds(dst, HALF), :],
+            s_ag2.at[idx], r_ag2.at[idx], ring[d],
+        )
+
+    def share(a, h, q):
         src = pl.ds(a * 2 * TOK + h * HALF, HALF)
         dst = pl.ds((a * 2 + 1) * TOK + h * HALF, HALF)
-        agc[a, h] = send(
-            norm2.at[src, :], norm2.at[dst, :], s_agc.at[a * 2 + h], r_agc.at[a * 2 + h], sib
-        )
-
+        idx = (a * 2 + h) * 2 + q
+        agc[a, h, q] = send(
+            norm2.at[q, src, :], norm2.at[q, dst, :], s_agc.at[idx], r_agc.at[idx], sib
+        )
+
+    sent = len(pending)
     for h in range(2):
         at = h * HALF
         value = stream[at : at + HALF, :] + rs_last(h, own2, rs2_recv, rs2)
+        scaled = normalize(value, gain2)
+        for q in range(2):
+            norm2[q, at : at + HALF, :] = scaled[:, q * WIDE : (q + 1) * WIDE]
+            for d in range(2):
+                ag2_send(d, 0, h, q)
         stream_out[at : at + HALF, :] = value.astype(BF)
-        norm2[at : at + HALF, :] = normalize(value, gain2)
-        for d in range(2):
-            ag2[d, 0, h] = ag_send(norm2, 2 * TOK, d, 0, h, s_ag2, r_ag2)
-        share(0, h)
+    for h in range(2):
+        for q in range(2):
+            share(0, h, q)
+    drain(sent)
 
     def ag2_pass(s):
         for h in range(2):
-            for d in range(2):
-                if (d, s, h) not in ag2:
-                    continue
-                ag2[d, s, h].wait_recv()
-                if s < 2 or (s == 2 and h == d):
-                    ag2[d, s + 1, h] = ag_send(norm2, 2 * TOK, d, s + 1, h, s_ag2, r_ag2)
-                share(AG_DST[d][s], h)
+            for q in range(2):
+                for d in range(2):
+                    if (d, s, h, q) not in ag2:
+                        continue
+                    ag2[d, s, h, q].wait_recv()
+                    if s < 2 or (s == 2 and h == d):
+                        ag2_send(d, s + 1, h, q)
+                    share(AG_DST[d][s], h, q)
 
     def project(first, last):
         for a in range(first, last + 1):
             for h in range(2):
-                agc[a, h].wait_recv()
+                for q in range(2):
+                    agc[a, h, q].wait_recv()
         lo, hi = first * 2 * TOK, (last + 1) * 2 * TOK
-        value = dot(norm2[lo:hi, :], wq[...]).astype(BF)
+        value = dot(norm2[0, lo:hi, :], wq[0:WIDE, :]) + dot(norm2[1, lo:hi, :], wq[WIDE:, :])
+        value = value.astype(BF)
         for a in range(first, last + 1):
             for par in range(2):
                 core = c if par == 0 else 1 - c
@@ -432,14 +461,11 @@
     project(1, 2)
     ag2_pass(2)
     project(3, 4)
+    project(5, 6)
     ag2_pass(3)
-    project(5, 6)
     project(7, 7)
 
-    for copy in pending:
-        copy.wait_send()
-    for k in range(1, NZ):
-        z_copy(k).wait_send()
+    drain(len(pending))
 
 
 def local(
@@ -457,9 +483,9 @@
         pltpu.VMEM((TOK, width), BF), pltpu.VMEM((1, width), F32), pltpu.VMEM((64, width), BF),
         pltpu.VMEM((8, TOK), jnp.int32), pltpu.VMEM((1, 64), F32), pltpu.VMEM((1, width), F32),
         pltpu.VMEM((256, width), F32), pltpu.VMEM((256, width), BF), pltpu.VMEM((256, width), BF),
-        pltpu.VMEM((256, width), BF), pltpu.VMEM((256, width), BF),
-        pltpu.VMEM((256, width), BF), pltpu.VMEM((256, width), BF),
-        pltpu.VMEM((256, width), BF), pltpu.VMEM((512, width), BF),
+        pltpu.VMEM((2, 256, WIDE), BF), pltpu.VMEM((2, 256, WIDE), BF),
+        pltpu.VMEM((2, 256, WIDE), BF), pltpu.VMEM((2, 256, WIDE), BF),
+        pltpu.VMEM((256, width), BF), pltpu.VMEM((2, 512, WIDE), BF),
         pltpu.VMEM((TOK, width), F32), pltpu.VMEM((256, width), F32),
         pltpu.VMEM((256, 128), BF), pltpu.VMEM((256, 384), F32), pltpu.VMEM((384, 256), BF),
         pltpu.VMEM((256, 384), BF),
@@ -468,9 +494,9 @@
         pltpu.VMEM((8, 128), F32), pltpu.VMEM((64, 128), F32),
         pltpu.VMEM((96, 128), F32),
         dma((12,)), dma((8,)), dma((8,)),
-        dma((16,)), dma((16,)), dma((16,)), dma((16,)),
-        dma((16,)), dma((16,)), dma((16,)), dma((16,)),
-        dma((16,)), dma((16,)), dma((8,)), dma((8,)),
+        dma((32,)), dma((32,)), dma((32,)), dma((32,)),
+        dma((16,)), dma((16,)), dma((32,)), dma((32,)),
+        dma((32,)), dma((32,)), dma((8,)), dma((8,)),
         dma((24,)), dma((24,)), dma((24,)), dma((24,)),
         dma((8,)), dma((8,)), dma((12,)), dma((12,)),
     ]

time: 110 us -> 107 us (0.973)
  Pallas kernels: 104 us -> 102 us
    pallas_call x1, Pallas kernels: 104 us -> 102 us  [local(): pl.pallas_call(kernel, out_shape=(jax.ShapeDtypeStruct((TOK, width), BF),...]
where the time goes in v3:
time: 107 us
  Pallas kernels  102 us (95%)
  local copies, waits for them, and re-layouts  4.35 us (4%)
    pallas_call x1, Pallas kernels, local(): pl.pallas_call(kernel, out_shape=(jax.ShapeDtypeStruct((TOK, width), BF),...  102 us
    unnamed x3, local copies, waits for them, and re-layouts  4.35 us

profile of v3, /device:TPU:1, one launch (start us, length us, event | category | flops | bytes accessed | tf_op | source)
XLA Modules:
  0.0 106.6 jit_solution(4303485780416028529)
XLA Ops:
  0.6 101.6 %shard_map.139 = (bf16[32,2048]{1,0:T(8,128)(2,1)}, bf16[512,256]{1,0:T(8,128)(2,1)}, f32[1,64]{1,0:T(1,128)}) custom-call(bf16[512,256]{1,0:T(8,128)(2,1)} %attn.1, bf16[256,2048]{1,0:T(8,128)(2,1)} %w_out.1, bf16[32,2048]{1,0:T(8,128)(2,1)} %residual_h.1, f32[1,2048]{1,0:T(1,128)} %bitcast.7, bf16[64,2048]{1,0:T(8,128)(2,1)} %bitcast.6, s32[8,32]{1,0:T(8,128)} %bitcast.9, ...), custom_call_target="tpu_custom_call" | custom-call | tf_op jit(solution)/shard_map/pallas_call | solution.py:503
  102.2 1.6 %copy.18 = bf16[32,2048]{1,0:T(8,128)(2,1)} copy(bf16[32,2048]{1,0:T(8,128)(2,1)} %get-tuple-element.12) | data formatting | bytes 262144
  103.8 1.7 %copy.19 = bf16[512,256]{1,0:T(8,128)(2,1)} copy(bf16[512,256]{1,0:T(8,128)(2,1)} %get-tuple-element.13) | data formatting | bytes 524288
  105.5 1.1 %copy.20 = f32[64]{0:T(128)} copy(f32[64]{0:T(128)} %bitcast.11) | data formatting | bytes 512

commit v4 on v3

--- a/solution.py
+++ b/solution.py
@@ -149,8 +149,10 @@
     load_bias = load(10, bias_h, bias)
     load_gain2 = load(11, gain2_h, gain2)
 
-    def rs_step(s, own, send_buf, recv_buf, ss, rs, copies):
+    def rs_step(s, own, send_buf, recv_buf, ss, rs, copies, upper_first=False):
         order = ((0, 0), (1, 1)) if s == 0 else ((0, 1), (1, 0), (0, 0), (1, 1))
+        if upper_first:
+            order = ((0, 0), (1, 0), (0, 1), (1, 1))
         for first in range(0, len(order), 2):
             for q in range(2):
                 for d, h in order[first : first + 2]:
@@ -332,10 +334,14 @@
             )
 
     for g in range(3):
+        if g == 2:
+            gone = [xs[2, dest] for dest in range(1, 8)]
+            for copy in gone:
+                copy.wait_send()
+            pending[:] = [copy for copy in pending if all(copy is not other for other in gone)]
+            give_back(0, (2, 3, 6, 7, 4))
         for dest in (2, 3, 6, 7, 4, 5, 1):
             xs[g, dest].wait_recv()
-        if g == 2:
-            give_back(0, (2, 3, 6, 7))
         arrived = x_recv[g * 128 : (g + 1) * 128, :]
         gate = dot(arrived, wg[...])
         upper = dot(arrived, wu[...])
@@ -348,7 +354,7 @@
     sent = len(pending)
     give_back(2, (4, 5, 2, 3, 6, 7, 1))
     give_back(1, (4, 5, 2, 3, 6, 7, 1))
-    give_back(0, (4, 5, 1))
+    give_back(0, (5, 1))
     for g in range(3):
         y_recv[g * 128 : g * 128 + HALF, :] = y_send[g * 128 : g * 128 + HALF, :]
     z_each(lambda k: z + k < NZ, lambda copy: copy.wait_recv())
@@ -381,7 +387,7 @@
     rs_step(1, own2, rs2_send, rs2_recv, s_rs2, r_rs2, rs2)
     rs_step(2, own2, rs2_send, rs2_recv, s_rs2, r_rs2, rs2)
     mixdown(0)
-    rs_step(3, own2, rs2_send, rs2_recv, s_rs2, r_rs2, rs2)
+    rs_step(3, own2, rs2_send, rs2_recv, s_rs2, r_rs2, rs2, upper_first=True)
 
     z_each(lambda k: z + k >= NZ, lambda copy: copy.wait_recv())
     total = cz[0:1, :]

time: 107 us -> 107 us (level)
  no operation moved by 1% of the time
where the time goes in v4:
time: 107 us; the launch traced here: 106 us
  Pallas kernels  101 us (94%)
  local copies, waits for them, and re-layouts  4.35 us (4%)
    pallas_call x1, Pallas kernels, local(): pl.pallas_call(kernel, out_shape=(jax.ShapeDtypeStruct((TOK, width), BF),...  101 us
    unnamed x3, local copies, waits for them, and re-layouts  4.35 us

profile of v4, /device:TPU:1, one launch (start us, length us, event | category | flops | bytes accessed | tf_op | source)
XLA Modules:
  0.0 106.5 jit_solution(14082440950207335462)
XLA Ops:
  0.6 101.5 %shard_map.139 = (bf16[32,2048]{1,0:T(8,128)(2,1)}, bf16[512,256]{1,0:T(8,128)(2,1)}, f32[1,64]{1,0:T(1,128)}) custom-call(bf16[512,256]{1,0:T(8,128)(2,1)} %attn.1, bf16[256,2048]{1,0:T(8,128)(2,1)} %w_out.1, bf16[32,2048]{1,0:T(8,128)(2,1)} %residual_h.1, f32[1,2048]{1,0:T(1,128)} %bitcast.7, bf16[64,2048]{1,0:T(8,128)(2,1)} %bitcast.6, s32[8,32]{1,0:T(8,128)} %bitcast.9, ...), custom_call_target="tpu_custom_call" | custom-call | tf_op jit(solution)/shard_map/pallas_call | solution.py:509
  102.1 1.6 %copy.18 = bf16[32,2048]{1,0:T(8,128)(2,1)} copy(bf16[32,2048]{1,0:T(8,128)(2,1)} %get-tuple-element.12) | data formatting | bytes 262144
  103.7 1.7 %copy.19 = bf16[512,256]{1,0:T(8,128)(2,1)} copy(bf16[512,256]{1,0:T(8,128)(2,1)} %get-tuple-element.13) | data formatting | bytes 524288
  105.4 1.1 %copy.20 = f32[64]{0:T(128)} copy(f32[64]{0:T(128)} %bitcast.11) | data formatting | bytes 512
